TPU v7x, 256 devices: a whole 4x4x8 slice. The times are simulated.
256 devices in a mesh: row: 32 (over y, z), col: 8 (over x, core).
Axes of the slice: x: 4, y: 4, z: 8, core: 2. Of those that a mesh axis runs over, the one named last changes fastest.
Arguments:
- tensor: float32 [32, 128, 256, 256], P(None, 'row', 'col'), may hold values from -21 to 21
- factor_y: float32 [256, 128], replicated, may hold values from -0.375 to 0.375
- factor_z: float32 [256, 128], replicated, may hold values from -0.375 to 0.375
- factor_s: float32 [32, 16], replicated, may hold values from -1 to 1
Outputs:
- core: float32 [16, 128, 128, 128], P(None, 'row', 'col')
- gram: float32 [128, 128], replicated
All inputs are finite; a program needn't handle non-finite values.
Results may differ from a plain program's by a relative error of at most 0.000086.
Values sent between devices are 32-bit elements; how exact they have to be, the bound alone decides.
A program may use at most 64 MiB of HBM per device.

v0:
```python
import jax
import jax.numpy as jnp
from jax import lax
from jax.sharding import PartitionSpec as P

RY = 128
RZ = 128
RS = 16


def body(tensor, factor_y, factor_z, factor_s):
    highest = lax.Precision.HIGHEST
    cells_y = tensor.shape[2]
    first = lax.axis_index("col") * cells_y
    rows_y = lax.dynamic_slice_in_dim(factor_y, first, cells_y, 0)
    reduced = jnp.einsum("sxyz,zc->sxyc", tensor, factor_z, precision=highest)
    reduced = jnp.einsum("sxyc,sr->rxyc", reduced, factor_s, precision=highest)
    partial_core = jnp.einsum("rxyc,yb->rxbc", reduced, rows_y, precision=highest)
    core = lax.psum_scatter(partial_core, "col", scatter_dimension=2, tiled=True)
    factor = jnp.float32(1.0 / (RY * RZ * RS))
    my_rows = jnp.einsum(
        "rxbc,rwbc->xw", core, lax.all_gather(core, "row", axis=1, tiled=True), precision=highest
    )
    my_rows = lax.psum(my_rows, "col") * factor
    gram = lax.all_gather(my_rows, "row", axis=0, tiled=True)
    return (core, gram)


def solution(mesh):
    in_specs = (P(None, "row", "col", None), P(), P(), P())
    out_specs = (P(None, "row", "col", None), P())
    return jax.shard_map(body, mesh=mesh, in_specs=in_specs, out_specs=out_specs, check_vma=False)
```

profile of v0, /device:TPU:8, one launch (start us, length us, event | category | flops | bytes accessed | tf_op | source)
XLA Modules:
  0.0 292.7 jit_solution(16011577386144129111)
XLA Ops:
  7.2 0.0 copy-start
  7.2 0.0 copy-start.1
  7.2 0.0 reduce-scatter.2.cloned.1.call-start
  7.2 5.7 %fusion.10 = f32[32,4,32,128]{3,2,1,0:T(8,128)S(1)} fusion(f32[32,4,32,256]{3,2,1,0:T(8,128)} %param.4, f32[256,128]{1,0:T(8,128)} %param.6), kind=kOutput, calls=%fused_computation.9 | convolution fusion | flops 1610612736 | bytes 6422528 | tf_op jit(solution)/shard_map/sxyz,zc->sxyc/dot_general | solution.py:16
  12.9 0.0 copy-done.1
  12.9 2.4 fusion.2
  15.3 0.0 copy-done
  15.3 5.1 %convolution_bitcast_fusion = f32[16,4,128,128]{3,2,1,0:T(8,128)} fusion(f32[4,32,128,16]{2,3,1,0:T(8,128)S(1)} %fusion.2, f32[256,128]{1,0:T(8,128)S(1)} %copy-done, s32[]{:T(128)S(6)} %select_n.3), kind=kOutput, calls=%fused_computation.2 | convolution fusion | flops 402653184 | bytes 5259268 | tf_op jit(solution)/shard_map/rxyc,yb->rxbc/dot_general | solution.py:18
  20.4 0.0 reduce-scatter.2.cloned.1.call-update
  20.4 0.0 all-gather.3.cloned.1.call-start
  20.5 43.5 %reduce-scatter.2.cloned.1.call-done = f32[16,4,16,128]{3,2,1,0:T(8,128)} async-done(((f32[16,4,128,128]{3,2,1,0:T(8,128)}), f32[16,4,16,128]{3,2,1,0:T(8,128)}) %reduce-scatter.2.cloned.1.call-update) | async-done | bytes 524304 | tf_op jit(solution)/shard_map/reduce_scatter | solution.py:19
  64.0 0.0 all-gather.3.cloned.1.call-update
  64.0 141.4 %all-gather.3.cloned.1.call-done = f32[16,128,16,128]{3,2,1,0:T(8,128)} async-done(((f32[16,4,16,128]{3,2,1,0:T(8,128)}), f32[16,128,16,128]{3,2,1,0:T(8,128)}) %all-gather.3.cloned.1.call-update) | async-done | bytes 16777232 | tf_op jit(solution)/shard_map/all_gather | solution.py:22
  205.4 18.4 %fusion.4 = f32[4,128]{1,0:T(4,128)S(1)} fusion(f32[16,128,16,128]{3,2,1,0:T(8,128)} %all-gather.3.cloned.1.call-done, f32[16,4,16,128]{3,2,1,0:T(8,128)} %reduce-scatter.2.cloned.1.call-done), kind=kOutput, calls=%fused_computation.5 | convolution fusion | flops 201326592 | bytes 17303552 | tf_op jit(solution)/shard_map/rxbc,rwbc->xw/dot_general | solution.py:21
  223.8 14.1 %psum.7 = f32[4,128]{1,0:T(4,128)S(1)} all-reduce(f32[4,128]{1,0:T(4,128)S(1)} %fusion.4), channel_id=1, replica_groups=mesh['row'=32,'col'=8] {'col'}, use_global_device_ids=true, to_apply=%region_1.0 | all-reduce | flops 512 | bytes 4096 | tf_op jit(solution)/shard_map/psum | solution.py:24
  237.9 47.3 %all-gather = f32[32,4,128]{2,1,0:T(4,128)S(1)} all-gather(f32[1,4,128]{2,1,0:T(4,128)S(1)} %multiply_bitcast_fusion), channel_id=1, replica_groups=mesh['row'=32,'col'=8] {'row'}, dimensions={0}, use_global_device_ids=true | all-gather | bytes 67584 | tf_op jit(solution)/shard_map/all_gather | solution.py:25
  285.3 0.6 copy.29
  (1 shorter events, 0.0 us)
Async XLA Ops:
  7.2 8.2 %copy-start = (f32[256,128]{1,0:T(8,128)S(1)}, f32[256,128]{1,0:T(8,128)}, u32[]{:S(2)}) copy-start(f32[256,128]{1,0:T(8,128)} %param.5) | copy-start | bytes 393220
  7.2 5.7 %copy-start.1 = (f32[32,16]{0,1:T(8,128)S(1)}, f32[32,16]{0,1:T(8,128)}, u32[]{:S(2)}) copy-start(f32[32,16]{0,1:T(8,128)} %param.7) | copy-start | bytes 6148
  7.2 56.8 %reduce-scatter.2.cloned.1.call-start = ((), (), s32[]{:S(2)}) async-start(), calls=%async_computation.1 | async-start | bytes 4718592 | tf_op jit(solution)/shard_map/reduce_scatter | solution.py:19
  20.4 185.0 %all-gather.3.cloned.1.call-start = ((), (), s32[]{:S(2)}) async-start(), calls=%async_computation.2 | async-start | bytes 17301504 | tf_op jit(solution)/shard_map/all_gather | solution.py:22
Sparse Core Ops, SparseCore 0:
  20.6 43.3 reduce-scatter.1
  67.1 138.2 all-gather.2
where the time goes:
time: 293 us
  waiting for transfers between devices  185 us (63%)
  blocking collectives  61.5 us (21%)
  matrix products  31.5 us (11%)
  between operations  14.1 us (5%)
    all_gather x1, waiting for transfers between devices, body(): lax.all_gather(core, 'row', axis=1, tiled=True)  141 us
    all_gather x1, blocking collectives, body(): gram = lax.all_gather(my_rows, 'row', axis=0, tiled=True)  47.3 us
    reduce_scatter x1, waiting for transfers between devices, body(): lax.psum_scatter(partial_core, 'col', scatter_dimension=2, tiled=True)  43.5 us
    dot_general x1, matrix products, body(): jnp.einsum('rxbc,rwbc->xw', core, lax.all_gather(core, 'row', axis=1, til...  18.4 us
    psum x1, blocking collectives, body(): my_rows = lax.psum(my_rows, 'col') * factor  14.1 us
  transfers between devices with their start and end apart: 2, of which 2 were waited for; matrix products, arithmetic and copies ran while one was open for 0% of the time, Pallas kernels for 0%

commit v1 on v0

v1 whole, which is shorter than its diff:
```python
import functools

import jax
import jax.numpy as jnp
from jax import lax
from jax.experimental import pallas as pl
from jax.experimental.pallas import tpu as pltpu
from jax.sharding import PartitionSpec as P

MESH = pl.DeviceIdType.MESH
F32 = jnp.float32
BF16 = jnp.bfloat16

SX, SY, SZ = 4, 4, 8
COLS, ROWS = 2 * SX, SY * SZ
S, NX, NY, NZ = 32, 4, 32, 256
R, B, C = 16, 128, 128
RL = R // COLS
BL = B // COLS
SCALE = 1.0 / (R * B * C)


def split(a):
    hi = a.astype(BF16)
    lo = (a - hi.astype(F32)).astype(BF16)
    return hi, lo


def dot(a, b):
    return jnp.dot(a, b, preferred_element_type=F32)


def dot_t(a, b):
    return lax.dot_general(a, b, (((1,), (1,)), ((), ())), preferred_element_type=F32)


def add_mod(a, d, n):
    return lax.rem(a + d, n)


def kernel(
    tensor, fy, fz, fs, core_out, gram_out,
    tbuf, send_r, recv_r, core, rows, part, buf_a, buf_b, fz_w, fy_w, fs_w,
    t_sem, s1, r1, s2, r2, so, ro, own_sem, s3, r3, s4, r4, s5, r5,
):
    i = lax.axis_index("row")
    j = lax.axis_index("col")
    y, z = i // SZ, lax.rem(i, SZ)
    x, k = j // 2, lax.rem(j, 2)

    def col_partner(d):
        return add_mod(j, d, COLS)

    def row_partner(d):
        return add_mod(i, d, ROWS)

    def zk_partner(d):
        zz, kk = add_mod(z, d // 2, SZ), add_mod(k, d % 2, 2)
        return zz, kk

    def xy_partner(d):
        return add_mod(x, d // SY, SX), add_mod(y, d % SY, SY)

    loads = [
        pltpu.make_async_copy(tensor.at[:, n], tbuf.at[n], t_sem.at[n]) for n in range(NX)
    ]
    for c in loads:
        c.start()

    barrier = pltpu.get_barrier_semaphore()

    def greet_row(d, _):
        pl.semaphore_signal(barrier, inc=1, device_id=(row_partner(d), j), device_id_type=MESH)
        return 0

    lax.fori_loop(1, ROWS, greet_row, 0)
    for d in range(1, COLS):
        pl.semaphore_signal(barrier, inc=1, device_id=(i, col_partner(d)), device_id_type=MESH)

    zh, zl = split(fz[...])
    fz_w[:, :C] = zh
    fz_w[:, C:] = zl
    yh, yl = split(fy[...].T)
    fy_w[:B] = yh
    fy_w[B:] = yl
    sh, sl = split(fs[...])
    pick_r = (
        lax.broadcasted_iota(jnp.int32, (R * 8, R), 0) // 8
        == lax.broadcasted_iota(jnp.int32, (R * 8, R), 1)
    ).astype(F32).astype(BF16)
    pick_s = (
        lax.broadcasted_iota(jnp.int32, (S, S * 8), 1) // 8
        == lax.broadcasted_iota(jnp.int32, (S, S * 8), 0)
    ).astype(F32).astype(BF16)
    same = (
        lax.broadcasted_iota(jnp.int32, (R * 8, S * 8), 0) % 8
        == lax.broadcasted_iota(jnp.int32, (R * 8, S * 8), 1) % 8
    )
    for part_s, at in ((sh, 0), (sl, R * 8)):
        wide = dot(dot_t(pick_r, part_s).astype(BF16), pick_s)
        fs_w[at : at + R * 8] = jnp.where(same, wide, 0.0).astype(BF16)

    for n in range(NX):
        loads[n].wait()
        for h in range(2):
            t = tbuf[n, :, 16 * h : 16 * h + 16, :].reshape(S * 16, NZ)
            th, tl = split(t)
            u = dot(th, fz_w[...])
            u = u[:, :C] + (u[:, C:] + dot(tl, fz_w[:, :C]))
            u = u.reshape(S, 2, 8, C)
            w = jnp.concatenate([u[:, 0].reshape(S * 8, C), u[:, 1].reshape(S * 8, C)], axis=1)
            wh, wl = split(w)
            v = dot(fs_w[...], wh)
            v = v[: R * 8] + (v[R * 8 :] + dot(fs_w[: R * 8], wl))
            for g in range(2):
                send_r[n, :, 16 * h + 8 * g : 16 * h + 8 * g + 8, :] = v[
                    :, g * C : (g + 1) * C
                ].reshape(R, 8, C)

    pl.semaphore_wait(barrier, ROWS - 1 + COLS - 1)

    mine_y = pl.ds(pl.multiple_of(j * NY, NY), NY)
    for n in range(NX):
        for d in range(1, COLS):
            q = col_partner(d)
            pltpu.make_async_remote_copy(
                src_ref=send_r.at[n, pl.ds(q * RL, RL)],
                dst_ref=recv_r.at[n, :, mine_y, :],
                send_sem=s1,
                recv_sem=r1.at[n],
                device_id=(i, q),
                device_id_type=MESH,
            ).start()
    for n in range(NX):
        recv_r[n, :, mine_y, :] = send_r[n, pl.ds(j * RL, RL)]

    for n in range(NX):
        got = recv_r.at[n, :, pl.ds(0, NY * (COLS - 1)), :]
        pltpu.make_async_copy(got, got, r1.at[n]).wait()
        m = jnp.concatenate([recv_r[n, 0], recv_r[n, 1]], axis=1)
        mh, ml = split(m)
        v = dot(fy_w[...], mh)
        v = v[:B] + (v[B:] + dot(fy_w[:B], ml))
        core[0, n] = v[:, :C]
        core[1, n] = v[:, C:]

        def send_rows(d, _, n=n):
            p = row_partner(d)
            pltpu.make_async_remote_copy(
                src_ref=core.at[p // 16, n, pl.ds(pl.multiple_of(lax.rem(p, 16) * 8, 8), 8), :],
                dst_ref=rows.at[i * NX + n],
                send_sem=s2,
                recv_sem=r2,
                device_id=(p, j),
                device_id_type=MESH,
            ).start()
            return 0

        lax.fori_loop(1, ROWS, send_rows, 0)
        rows[i * NX + n] = core[i // 16, n, pl.ds(pl.multiple_of(lax.rem(i, 16) * 8, 8), 8), :]

    for d in range(1, COLS):
        q = col_partner(d)
        pltpu.make_async_remote_copy(
            src_ref=core.at[:, :, pl.ds(pl.multiple_of(q * BL, BL), BL), :],
            dst_ref=core_out.at[pl.ds(j * RL, RL)],
            send_sem=so,
            recv_sem=ro,
            device_id=(i, q),
            device_id_type=MESH,
        ).start()
    own = pltpu.make_async_copy(
        core.at[:, :, pl.ds(pl.multiple_of(j * BL, BL), BL), :],
        core_out.at[pl.ds(j * RL, RL)],
        own_sem,
    )
    own.start()

    got = rows.at[pl.ds(0, (ROWS - 1) * NX)]
    pltpu.make_async_copy(got, got, r2).wait()
    gh, gl = [], []
    for e in range(8):
        h, l = split(rows[:, e, :])
        gh.append(h)
        gl.append(l)
    gh = jnp.concatenate(gh, axis=1)
    gl = jnp.concatenate(gl, axis=1)
    cross = dot_t(gh, gl)
    part[...] = (dot_t(gh, gh) + (cross + cross.T)).reshape(16, 8, 128)

    mine = z * 2 + k
    for d in range(1, 16):
        zz, kk = zk_partner(d)
        pltpu.make_async_remote_copy(
            src_ref=part.at[zz * 2 + kk],
            dst_ref=buf_a.at[mine],
            send_sem=s3,
            recv_sem=r3,
            device_id=(y * SZ + zz, x * 2 + kk),
            device_id_type=MESH,
        ).start()
    buf_a[mine] = part[mine]
    pltpu.make_async_copy(buf_a.at[pl.ds(0, 15)], buf_a.at[pl.ds(0, 15)], r3).wait()
    total = jnp.sum(buf_a[...], axis=0)

    at_xy = x * SY + y
    buf_b[at_xy] = total
    for d in range(1, 16):
        xx, yy = xy_partner(d)
        pltpu.make_async_remote_copy(
            src_ref=buf_b.at[at_xy],
            dst_ref=buf_b.at[at_xy],
            send_sem=s4,
            recv_sem=r4,
            device_id=(yy * SZ + z, xx * 2 + k),
            device_id_type=MESH,
        ).start()
    pltpu.make_async_copy(buf_b.at[pl.ds(0, 15)], buf_b.at[pl.ds(0, 15)], r4).wait()
    gram_out[mine] = jnp.sum(buf_b[...], axis=0) * SCALE

    for d in range(1, 16):
        zz, kk = zk_partner(d)
        pltpu.make_async_remote_copy(
            src_ref=gram_out.at[mine],
            dst_ref=gram_out.at[mine],
            send_sem=s5,
            recv_sem=r5,
            device_id=(y * SZ + zz, x * 2 + kk),
            device_id_type=MESH,
        ).start()

    sent = send_r.at[:, pl.ds(0, R - RL)]
    pltpu.make_async_copy(sent, sent, s1).wait()
    sent = rows.at[pl.ds(0, (ROWS - 1) * NX)]
    pltpu.make_async_copy(sent, sent, s2).wait()
    sent = core.at[:, :, pl.ds(0, B - BL), :]
    pltpu.make_async_copy(sent, sent, so).wait()
    own.wait()
    for sem in (s3, s4, s5):
        pltpu.make_async_copy(buf_a.at[pl.ds(0, 15)], buf_a.at[pl.ds(0, 15)], sem).wait()
    got = core_out.at[pl.ds(0, R - RL)]
    pltpu.make_async_copy(got, got, ro).wait()
    pltpu.make_async_copy(gram_out.at[pl.ds(0, 15)], gram_out.at[pl.ds(0, 15)], r5).wait()


def body(tensor, factor_y, factor_z, factor_s):
    dma = pltpu.SemaphoreType.DMA
    core, gram = pl.pallas_call(
        kernel,
        out_shape=(
            jax.ShapeDtypeStruct((R, NX, BL, C), F32),
            jax.ShapeDtypeStruct((16, 8, 128), F32),
        ),
        in_specs=[pl.BlockSpec(memory_space=pl.ANY)] + [pl.BlockSpec(memory_space=pltpu.VMEM)] * 3,
        out_specs=(pl.BlockSpec(memory_space=pl.ANY), pl.BlockSpec(memory_space=pltpu.VMEM)),
        scratch_shapes=[
            pltpu.VMEM((NX, S, NY, NZ), F32),
            pltpu.VMEM((NX, R, NY, C), F32),
            pltpu.VMEM((NX, RL, NY * COLS, C), F32),
            pltpu.VMEM((RL, NX, B, C), F32),
            pltpu.VMEM((ROWS * NX, 8, C), F32),
            pltpu.VMEM((16, 8, 128), F32),
            pltpu.VMEM((16, 8, 128), F32),
            pltpu.VMEM((16, 8, 128), F32),
            pltpu.VMEM((NZ, 2 * C), BF16),
            pltpu.VMEM((2 * B, NY * COLS), BF16),
            pltpu.VMEM((2 * R * 8, S * 8), BF16),
            dma((NX,)),
            dma, dma((NX,)),
            dma, dma,
            dma, dma, dma,
            dma, dma,
            dma, dma,
            dma, dma,
        ],
        compiler_params=pltpu.CompilerParams(
            collective_id=0, has_side_effects=True, vmem_limit_bytes=48 * 1024 * 1024
        ),
    )(tensor, factor_y, factor_z, factor_s)
    return core, gram.reshape(128, 128)


def solution(mesh):
    in_specs = (P(None, "row", "col", None), P(), P(), P())
    out_specs = (P(None, "row", "col", None), P())
    return jax.shard_map(body, mesh=mesh, in_specs=in_specs, out_specs=out_specs, check_vma=False)
```

time: 293 us -> 56.8 us (0.19)
  the two profiles are of different devices: /device:TPU:8 before, /device:TPU:1 now
where the time goes in v1:
time: 56.8 us; the launch traced here: 56.6 us
  Pallas kernels  49.8 us (88%)
  local copies, waits for them, and re-layouts  6.19 us (11%)
  between operations  0.64 us (1%)
    pallas_call x1, Pallas kernels, body(): pl.pallas_call(kernel, out_shape=(jax.ShapeDtypeStruct((R, NX, BL, C), F3...  49.8 us
    unnamed x9, local copies, waits for them, and re-layouts  6.19 us

profile of v1, /device:TPU:1, one launch (start us, length us, event | category | flops | bytes accessed | tf_op | source)
XLA Modules:
  0.0 56.6 jit_solution(9869753820079974364)
XLA Ops:
  0.6 0.8 %copy.6.fs = f32[32,16]{1,0:T(8,128)S(1)} copy(f32[32,16]{0,1:T(8,128)} %param.7) | data formatting | bytes 4096 | tf_op args[3]
  1.4 0.0 copy-start
  1.4 2.2 %copy-done = f32[32,4,32,256]{3,2,1,0:T(8,128)S(1)} copy-done((f32[32,4,32,256]{3,2,1,0:T(8,128)S(1)}, f32[32,4,32,256]{3,2,1,0:T(8,128)}, u32[]{:S(2)}) %copy-start) | copy-done | bytes 4194328
  3.6 0.0 copy-start.1
  3.6 0.9 %copy-done.1 = f32[256,128]{1,0:T(8,128)S(1)} copy-done((f32[256,128]{1,0:T(8,128)S(1)}, f32[256,128]{1,0:T(8,128)}, u32[]{:S(2)}) %copy-start.1) | copy-done | bytes 131096
  4.5 0.0 copy-start.2
  4.5 0.9 %copy-done.2 = f32[256,128]{1,0:T(8,128)S(1)} copy-done((f32[256,128]{1,0:T(8,128)S(1)}, f32[256,128]{1,0:T(8,128)}, u32[]{:S(2)}) %copy-start.2) | copy-done | bytes 131096
  5.4 49.8 %shard_map.59 = (f32[16,4,16,128]{3,2,1,0:T(8,128)S(1)}, f32[16,8,128]{2,1,0:T(8,128)S(1)}) custom-call(f32[32,4,32,256]{3,2,1,0:T(8,128)S(1)} %copy-done, f32[256,128]{1,0:T(8,128)S(1)} %copy-done.1, f32[256,128]{1,0:T(8,128)S(1)} %copy-done.2, f32[32,16]{1,0:T(8,128)S(1)} %copy.6.fs), custom_call_target="tpu_custom_call" | custom-call | tf_op jit(solution)/shard_map/pallas_call | solution.py:248
  55.2 0.8 %copy.9 = f32[16,4,16,128]{3,2,1,0:T(8,128)} copy(f32[16,4,16,128]{3,2,1,0:T(8,128)S(1)} %get-tuple-element.8) | data formatting | bytes 1048576
  56.0 0.6 %copy.10 = f32[128,128]{1,0:T(8,128)} copy(f32[128,128]{1,0:T(8,128)S(1)} %bitcast.1) | data formatting | bytes 131072
Async XLA Ops:
  1.4 2.2 %copy-start = (f32[32,4,32,256]{3,2,1,0:T(8,128)S(1)}, f32[32,4,32,256]{3,2,1,0:T(8,128)}, u32[]{:S(2)}) copy-start(f32[32,4,32,256]{3,2,1,0:T(8,128)} %tensor.1) | copy-start | bytes 12582916
  3.6 0.9 %copy-start.1 = (f32[256,128]{1,0:T(8,128)S(1)}, f32[256,128]{1,0:T(8,128)}, u32[]{:S(2)}) copy-start(f32[256,128]{1,0:T(8,128)} %fy.1) | copy-start | bytes 393220
  4.5 0.9 %copy-start.2 = (f32[256,128]{1,0:T(8,128)S(1)}, f32[256,128]{1,0:T(8,128)}, u32[]{:S(2)}) copy-start(f32[256,128]{1,0:T(8,128)} %fz.1) | copy-start | bytes 393220

commit v2 on v1

--- a/solution.py
+++ b/solution.py
@@ -18,6 +18,7 @@
 RL = R // COLS
 BL = B // COLS
 SCALE = 1.0 / (R * B * C)
+VMEM_BYTES = 63 * 1024 * 1024
 
 
 def split(a):
@@ -39,9 +40,9 @@
 
 
 def kernel(
-    tensor, fy, fz, fs, core_out, gram_out,
-    tbuf, send_r, recv_r, core, rows, part, buf_a, buf_b, fz_w, fy_w, fs_w,
-    t_sem, s1, r1, s2, r2, so, ro, own_sem, s3, r3, s4, r4, s5, r5,
+    tensor, fy_hbm, fz_hbm, fs_hbm, core_out, gram_out,
+    fy, fz, fs, tbuf, send_r, recv_r, core, rows, part, buf_a, buf_b, fz_w, fy_w, fs_w,
+    f_sem, t_sem, s1, r1, s2, r2, so, ro, own_sem, s3, r3, s4, r4, s5, r5,
 ):
     i = lax.axis_index("row")
     j = lax.axis_index("col")
@@ -64,7 +65,11 @@
     loads = [
         pltpu.make_async_copy(tensor.at[:, n], tbuf.at[n], t_sem.at[n]) for n in range(NX)
     ]
-    for c in loads:
+    factors = [
+        pltpu.make_async_copy(a, b, f_sem.at[n])
+        for n, (a, b) in enumerate(((fz_hbm, fz), (fs_hbm, fs), (fy_hbm, fy)))
+    ]
+    for c in factors[:2] + loads[:1] + factors[2:] + loads[1:]:
         c.start()
 
     barrier = pltpu.get_barrier_semaphore()
@@ -77,6 +82,8 @@
     for d in range(1, COLS):
         pl.semaphore_signal(barrier, inc=1, device_id=(i, col_partner(d)), device_id_type=MESH)
 
+    for c in factors:
+        c.wait()
     zh, zl = split(fz[...])
     fz_w[:, :C] = zh
     fz_w[:, C:] = zl
@@ -97,7 +104,7 @@
         == lax.broadcasted_iota(jnp.int32, (R * 8, S * 8), 1) % 8
     )
     for part_s, at in ((sh, 0), (sl, R * 8)):
-        wide = dot(dot_t(pick_r, part_s).astype(BF16), pick_s)
+        wide = dot(dot(pick_r, part_s).astype(BF16), pick_s)
         fs_w[at : at + R * 8] = jnp.where(same, wide, 0.0).astype(BF16)
 
     for n in range(NX):
@@ -251,9 +258,12 @@
             jax.ShapeDtypeStruct((R, NX, BL, C), F32),
             jax.ShapeDtypeStruct((16, 8, 128), F32),
         ),
-        in_specs=[pl.BlockSpec(memory_space=pl.ANY)] + [pl.BlockSpec(memory_space=pltpu.VMEM)] * 3,
+        in_specs=[pl.BlockSpec(memory_space=pl.ANY)] * 4,
         out_specs=(pl.BlockSpec(memory_space=pl.ANY), pl.BlockSpec(memory_space=pltpu.VMEM)),
         scratch_shapes=[
+            pltpu.VMEM((NY * COLS, B), F32),
+            pltpu.VMEM((NZ, C), F32),
+            pltpu.VMEM((R, S), F32),
             pltpu.VMEM((NX, S, NY, NZ), F32),
             pltpu.VMEM((NX, R, NY, C), F32),
             pltpu.VMEM((NX, RL, NY * COLS, C), F32),
@@ -265,6 +275,7 @@
             pltpu.VMEM((NZ, 2 * C), BF16),
             pltpu.VMEM((2 * B, NY * COLS), BF16),
             pltpu.VMEM((2 * R * 8, S * 8), BF16),
+            dma((3,)),
             dma((NX,)),
             dma, dma((NX,)),
             dma, dma,
@@ -274,9 +285,9 @@
             dma, dma,
         ],
         compiler_params=pltpu.CompilerParams(
-            collective_id=0, has_side_effects=True, vmem_limit_bytes=48 * 1024 * 1024
+            collective_id=0, has_side_effects=True, vmem_limit_bytes=VMEM_BYTES
         ),
-    )(tensor, factor_y, factor_z, factor_s)
+    )(tensor, factor_y, factor_z, factor_s.T)
     return core, gram.reshape(128, 128)
 
 

time: 56.8 us -> 56.2 us (0.989)
  local copies, waits for them, and re-layouts: 6.19 us -> 3.35 us
  Pallas kernels: 49.8 us -> 52.1 us
    unnamed x9 -> x2, local copies, waits for them, and re-layouts: 6.19 us -> 3.35 us
    pallas_call x1, Pallas kernels: 49.8 us -> 52.1 us  [body(): pl.pallas_call(kernel, out_shape=(jax.ShapeDtypeStruct((R, NX, BL, C), F3...]
where the time goes in v2:
time: 56.2 us; the launch traced here: 56.1 us
  Pallas kernels  52.1 us (93%)
  local copies, waits for them, and re-layouts  3.35 us (6%)
  between operations  0.64 us (1%)
    pallas_call x1, Pallas kernels, body(): pl.pallas_call(kernel, out_shape=(jax.ShapeDtypeStruct((R, NX, BL, C), F3...  52.1 us
    unnamed x2, local copies, waits for them, and re-layouts  3.35 us

profile of v2, /device:TPU:1, one launch (start us, length us, event | category | flops | bytes accessed | tf_op | source)
XLA Modules:
  0.0 56.1 jit_solution(6085971435773726449)
XLA Ops:
  0.6 52.1 %shard_map.59 = (f32[16,4,16,128]{3,2,1,0:T(8,128)}, f32[16,8,128]{2,1,0:T(8,128)}) custom-call(f32[32,4,32,256]{3,2,1,0:T(8,128)} %tensor.1, f32[256,128]{1,0:T(8,128)} %fy_hbm.1, f32[256,128]{1,0:T(8,128)} %fz_hbm.1, f32[16,32]{1,0:T(8,128)} %bitcast.3), custom_call_target="tpu_custom_call" | custom-call | tf_op jit(solution)/shard_map/pallas_call | solution.py:255
  52.7 1.9 %copy.8 = f32[16,4,16,128]{3,2,1,0:T(8,128)} copy(f32[16,4,16,128]{3,2,1,0:T(8,128)} %get-tuple-element.8) | data formatting | bytes 1048576
  54.6 1.5 %copy.9 = f32[128,128]{1,0:T(8,128)} copy(f32[128,128]{1,0:T(8,128)} %bitcast.2) | data formatting | bytes 131072

commit v3 on v2

--- a/solution.py
+++ b/solution.py
@@ -42,7 +42,7 @@
 def kernel(
     tensor, fy_hbm, fz_hbm, fs_hbm, core_out, gram_out,
     fy, fz, fs, tbuf, send_r, recv_r, core, rows, part, buf_a, buf_b, fz_w, fy_w, fs_w,
-    f_sem, t_sem, s1, r1, s2, r2, so, ro, own_sem, s3, r3, s4, r4, s5, r5,
+    group_in, rows_in, f_sem, t_sem, s1, r1, s2, r2, so, ro, own_sem, s3, r3, s4, r4, s5, r5,
 ):
     i = lax.axis_index("row")
     j = lax.axis_index("col")
@@ -73,14 +73,12 @@
         c.start()
 
     barrier = pltpu.get_barrier_semaphore()
-
-    def greet_row(d, _):
-        pl.semaphore_signal(barrier, inc=1, device_id=(row_partner(d), j), device_id_type=MESH)
-        return 0
-
-    lax.fori_loop(1, ROWS, greet_row, 0)
-    for d in range(1, COLS):
-        pl.semaphore_signal(barrier, inc=1, device_id=(i, col_partner(d)), device_id_type=MESH)
+    for q in range(COLS):
+        if q != 1:
+
+            @pl.when(j != q)
+            def _():
+                pl.semaphore_signal(barrier, inc=1, device_id=(i, q), device_id_type=MESH)
 
     for c in factors:
         c.wait()
@@ -107,6 +105,7 @@
         wide = dot(dot(pick_r, part_s).astype(BF16), pick_s)
         fs_w[at : at + R * 8] = jnp.where(same, wide, 0.0).astype(BF16)
 
+    mine_y = pl.ds(pl.multiple_of(j * NY, NY), NY)
     for n in range(NX):
         loads[n].wait()
         for h in range(2):
@@ -123,11 +122,28 @@
                 send_r[n, :, 16 * h + 8 * g : 16 * h + 8 * g + 8, :] = v[
                     :, g * C : (g + 1) * C
                 ].reshape(R, 8, C)
-
-    pl.semaphore_wait(barrier, ROWS - 1 + COLS - 1)
-
-    mine_y = pl.ds(pl.multiple_of(j * NY, NY), NY)
-    for n in range(NX):
+        if n == 0:
+
+            @pl.when(j != 1)
+            def _():
+                pl.semaphore_wait(barrier, COLS - 1)
+
+            @pl.when(j == 0)
+            def _():
+                pl.semaphore_signal(group_in, inc=1, device_id=(i, 1), device_id_type=MESH)
+
+                def greet_row(d, _):
+                    pl.semaphore_signal(
+                        barrier, inc=1, device_id=(row_partner(d), 1), device_id_type=MESH
+                    )
+                    return 0
+
+                lax.fori_loop(1, ROWS, greet_row, 0)
+
+            @pl.when(j == 1)
+            def _():
+                pl.semaphore_wait(group_in, 1)
+
         for d in range(1, COLS):
             q = col_partner(d)
             pltpu.make_async_remote_copy(
@@ -138,6 +154,14 @@
                 device_id=(i, q),
                 device_id_type=MESH,
             ).start()
+
+    @pl.when(j == 1)
+    def _():
+        pl.semaphore_wait(barrier, ROWS - 1)
+        for q in range(COLS):
+            if q != 1:
+                pl.semaphore_signal(rows_in, inc=1, device_id=(i, q), device_id_type=MESH)
+
     for n in range(NX):
         recv_r[n, :, mine_y, :] = send_r[n, pl.ds(j * RL, RL)]
 
@@ -150,6 +174,12 @@
         v = v[:B] + (v[B:] + dot(fy_w[:B], ml))
         core[0, n] = v[:, :C]
         core[1, n] = v[:, C:]
+
+        if n == 0:
+
+            @pl.when(j != 1)
+            def _():
+                pl.semaphore_wait(rows_in, 1)
 
         def send_rows(d, _, n=n):
             p = row_partner(d)
@@ -275,6 +305,8 @@
             pltpu.VMEM((NZ, 2 * C), BF16),
             pltpu.VMEM((2 * B, NY * COLS), BF16),
             pltpu.VMEM((2 * R * 8, S * 8), BF16),
+            pltpu.SemaphoreType.REGULAR,
+            pltpu.SemaphoreType.REGULAR,
             dma((3,)),
             dma((NX,)),
             dma, dma((NX,)),

time: 56.2 us -> 53.3 us (0.948)
  Pallas kernels: 52.1 us -> 49.1 us
    pallas_call x1, Pallas kernels: 52.1 us -> 49.1 us  [body(): pl.pallas_call(kernel, out_shape=(jax.ShapeDtypeStruct((R, NX, BL, C), F3...]
where the time goes in v3:
time: 53.3 us; the launch traced here: 53.1 us
  Pallas kernels  49.1 us (92%)
  local copies, waits for them, and re-layouts  3.35 us (6%)
  between operations  0.64 us (1%)
    pallas_call x1, Pallas kernels, body(): pl.pallas_call(kernel, out_shape=(jax.ShapeDtypeStruct((R, NX, BL, C), F3...  49.1 us
    unnamed x2, local copies, waits for them, and re-layouts  3.35 us

profile of v3, /device:TPU:1, one launch (start us, length us, event | category | flops | bytes accessed | tf_op | source)
XLA Modules:
  0.0 53.1 jit_solution(10520005778825054418)
XLA Ops:
  0.6 49.1 %shard_map.59 = (f32[16,4,16,128]{3,2,1,0:T(8,128)}, f32[16,8,128]{2,1,0:T(8,128)}) custom-call(f32[32,4,32,256]{3,2,1,0:T(8,128)} %tensor.1, f32[256,128]{1,0:T(8,128)} %fy_hbm.1, f32[256,128]{1,0:T(8,128)} %fz_hbm.1, f32[16,32]{1,0:T(8,128)} %bitcast.3), custom_call_target="tpu_custom_call" | custom-call | tf_op jit(solution)/shard_map/pallas_call | solution.py:285
  49.8 1.9 %copy.8 = f32[16,4,16,128]{3,2,1,0:T(8,128)} copy(f32[16,4,16,128]{3,2,1,0:T(8,128)} %get-tuple-element.8) | data formatting | bytes 1048576
  51.7 1.5 %copy.9 = f32[128,128]{1,0:T(8,128)} copy(f32[128,128]{1,0:T(8,128)} %bitcast.2) | data formatting | bytes 131072

commit v4 on v2

--- a/solution.py
+++ b/solution.py
@@ -18,6 +18,7 @@
 RL = R // COLS
 BL = B // COLS
 SCALE = 1.0 / (R * B * C)
+FAR_FIRST = (4, 5, 3, 2, 6, 7, 1)
 VMEM_BYTES = 63 * 1024 * 1024
 
 
@@ -41,8 +42,8 @@
 
 def kernel(
     tensor, fy_hbm, fz_hbm, fs_hbm, core_out, gram_out,
-    fy, fz, fs, tbuf, send_r, recv_r, core, rows, part, buf_a, buf_b, fz_w, fy_w, fs_w,
-    f_sem, t_sem, s1, r1, s2, r2, so, ro, own_sem, s3, r3, s4, r4, s5, r5,
+    fy, fz, fs, tbuf, send_r, recv_r, core, rows, part, buf_a, buf_b, total, fz_w, fy_w, fs_w,
+    mate_in, f_sem, t_sem, s1, r1, s2, r2, so, ro, own_sem, s3, r3, s4, r4, s5, r5,
 ):
     i = lax.axis_index("row")
     j = lax.axis_index("col")
@@ -54,13 +55,6 @@
 
     def row_partner(d):
         return add_mod(i, d, ROWS)
-
-    def zk_partner(d):
-        zz, kk = add_mod(z, d // 2, SZ), add_mod(k, d % 2, 2)
-        return zz, kk
-
-    def xy_partner(d):
-        return add_mod(x, d // SY, SX), add_mod(y, d % SY, SY)
 
     loads = [
         pltpu.make_async_copy(tensor.at[:, n], tbuf.at[n], t_sem.at[n]) for n in range(NX)
@@ -74,13 +68,25 @@
 
     barrier = pltpu.get_barrier_semaphore()
 
+    def greet_col(d, _):
+        pl.semaphore_signal(
+            barrier, inc=1, device_id=(i, 2 * add_mod(x, d, SX)), device_id_type=MESH
+        )
+        return 0
+
     def greet_row(d, _):
-        pl.semaphore_signal(barrier, inc=1, device_id=(row_partner(d), j), device_id_type=MESH)
+        pl.semaphore_signal(
+            barrier, inc=1, device_id=(row_partner(d), 2 * x + 1), device_id_type=MESH
+        )
         return 0
 
+    for d in range(SX):
+
+        @pl.when(k + d > 0)
+        def _():
+            greet_col(d, 0)
+
     lax.fori_loop(1, ROWS, greet_row, 0)
-    for d in range(1, COLS):
-        pl.semaphore_signal(barrier, inc=1, device_id=(i, col_partner(d)), device_id_type=MESH)
 
     for c in factors:
         c.wait()
@@ -107,6 +113,7 @@
         wide = dot(dot(pick_r, part_s).astype(BF16), pick_s)
         fs_w[at : at + R * 8] = jnp.where(same, wide, 0.0).astype(BF16)
 
+    mine_y = pl.ds(pl.multiple_of(j * NY, NY), NY)
     for n in range(NX):
         loads[n].wait()
         for h in range(2):
@@ -123,48 +130,71 @@
                 send_r[n, :, 16 * h + 8 * g : 16 * h + 8 * g + 8, :] = v[
                     :, g * C : (g + 1) * C
                 ].reshape(R, 8, C)
-
-    pl.semaphore_wait(barrier, ROWS - 1 + COLS - 1)
-
-    mine_y = pl.ds(pl.multiple_of(j * NY, NY), NY)
-    for n in range(NX):
-        for d in range(1, COLS):
-            q = col_partner(d)
-            pltpu.make_async_remote_copy(
-                src_ref=send_r.at[n, pl.ds(q * RL, RL)],
-                dst_ref=recv_r.at[n, :, mine_y, :],
-                send_sem=s1,
-                recv_sem=r1.at[n],
-                device_id=(i, q),
-                device_id_type=MESH,
-            ).start()
+        if n == 0:
+
+            @pl.when(k == 0)
+            def _():
+                pl.semaphore_wait(barrier, COLS - 1)
+                pl.semaphore_signal(mate_in, inc=1, device_id=(i, j + 1), device_id_type=MESH)
+
+            @pl.when(k == 1)
+            def _():
+                pl.semaphore_wait(mate_in, 1)
+
+        for rank in range(RL):
+            for d in FAR_FIRST:
+                q = col_partner(d)
+                pltpu.make_async_remote_copy(
+                    src_ref=send_r.at[n, q * RL + rank],
+                    dst_ref=recv_r.at[n, rank, mine_y, :],
+                    send_sem=s1,
+                    recv_sem=r1.at[n, rank],
+                    device_id=(i, q),
+                    device_id_type=MESH,
+                ).start()
+
+    @pl.when(k == 1)
+    def _():
+        pl.semaphore_wait(barrier, 2 * (ROWS - 1))
+        pl.semaphore_signal(mate_in, inc=1, device_id=(i, j - 1), device_id_type=MESH)
+
     for n in range(NX):
         recv_r[n, :, mine_y, :] = send_r[n, pl.ds(j * RL, RL)]
 
+    def block(p):
+        return pl.ds(pl.multiple_of(p // RL * 8, 8), 8)
+
     for n in range(NX):
-        got = recv_r.at[n, :, pl.ds(0, NY * (COLS - 1)), :]
-        pltpu.make_async_copy(got, got, r1.at[n]).wait()
-        m = jnp.concatenate([recv_r[n, 0], recv_r[n, 1]], axis=1)
-        mh, ml = split(m)
-        v = dot(fy_w[...], mh)
-        v = v[:B] + (v[B:] + dot(fy_w[:B], ml))
-        core[0, n] = v[:, :C]
-        core[1, n] = v[:, C:]
-
-        def send_rows(d, _, n=n):
-            p = row_partner(d)
-            pltpu.make_async_remote_copy(
-                src_ref=core.at[p // 16, n, pl.ds(pl.multiple_of(lax.rem(p, 16) * 8, 8), 8), :],
-                dst_ref=rows.at[i * NX + n],
-                send_sem=s2,
-                recv_sem=r2,
-                device_id=(p, j),
-                device_id_type=MESH,
-            ).start()
-            return 0
-
-        lax.fori_loop(1, ROWS, send_rows, 0)
-        rows[i * NX + n] = core[i // 16, n, pl.ds(pl.multiple_of(lax.rem(i, 16) * 8, 8), 8), :]
+        for rank in range(RL):
+            got = recv_r.at[n, rank, pl.ds(0, NY * (COLS - 1)), :]
+            pltpu.make_async_copy(got, got, r1.at[n, rank]).wait()
+            mh, ml = split(recv_r[n, rank])
+            v = dot(fy_w[...], mh)
+            core[rank, n] = v[:B] + (v[B:] + dot(fy_w[:B], ml))
+            if n == 0 and rank == 0:
+
+                @pl.when(k == 0)
+                def _():
+                    pl.semaphore_wait(mate_in, 1)
+
+            def send_rows(d, _, n=n, rank=rank):
+                p = lax.rem(i // RL + d, ROWS // RL) * RL + rank
+
+                @pl.when(p != i)
+                def _():
+                    pltpu.make_async_remote_copy(
+                        src_ref=core.at[rank, n, block(p), :],
+                        dst_ref=rows.at[i * NX + n],
+                        send_sem=s2,
+                        recv_sem=r2,
+                        device_id=(p, j),
+                        device_id_type=MESH,
+                    ).start()
+
+                return 0
+
+            lax.fori_loop(0, ROWS // RL, send_rows, 0)
+        rows[i * NX + n] = core[lax.rem(i, RL), n, block(i), :]
 
     for d in range(1, COLS):
         q = col_partner(d)
@@ -179,7 +209,7 @@
     own = pltpu.make_async_copy(
         core.at[:, :, pl.ds(pl.multiple_of(j * BL, BL), BL), :],
         core_out.at[pl.ds(j * RL, RL)],
-        own_sem,
+        own_sem.at[0],
     )
     own.start()
 
@@ -192,49 +222,57 @@
         gl.append(l)
     gh = jnp.concatenate(gh, axis=1)
     gl = jnp.concatenate(gl, axis=1)
-    cross = dot_t(gh, gl)
-    part[...] = (dot_t(gh, gh) + (cross + cross.T)).reshape(16, 8, 128)
-
-    mine = z * 2 + k
+    g = dot_t(jnp.concatenate([gh, gl], axis=0), gh)
+    cross = g[128:]
+    part[...] = (g[:128] + (cross + cross.T)).reshape(16, 8, 128)
+
+    at_xy, at_zk = x * SY + y, z * 2 + k
+
+    def over_xy(d):
+        xx, yy = add_mod(x, d // SY, SX), add_mod(y, d % SY, SY)
+        return xx * SY + yy, (yy * SZ + z, xx * 2 + k)
+
+    def over_zk(d):
+        zz, kk = add_mod(z, d // 2, SZ), add_mod(k, d % 2, 2)
+        return (y * SZ + zz, x * 2 + kk)
+
     for d in range(1, 16):
-        zz, kk = zk_partner(d)
+        slot, device = over_xy(d)
         pltpu.make_async_remote_copy(
-            src_ref=part.at[zz * 2 + kk],
-            dst_ref=buf_a.at[mine],
+            src_ref=part.at[slot],
+            dst_ref=buf_a.at[at_xy],
             send_sem=s3,
             recv_sem=r3,
-            device_id=(y * SZ + zz, x * 2 + kk),
+            device_id=device,
             device_id_type=MESH,
         ).start()
-    buf_a[mine] = part[mine]
+    buf_a[at_xy] = part[at_xy]
     pltpu.make_async_copy(buf_a.at[pl.ds(0, 15)], buf_a.at[pl.ds(0, 15)], r3).wait()
-    total = jnp.sum(buf_a[...], axis=0)
-
-    at_xy = x * SY + y
-    buf_b[at_xy] = total
+
+    buf_b[at_zk] = jnp.sum(buf_a[...], axis=0)
     for d in range(1, 16):
-        xx, yy = xy_partner(d)
         pltpu.make_async_remote_copy(
-            src_ref=buf_b.at[at_xy],
-            dst_ref=buf_b.at[at_xy],
+            src_ref=buf_b.at[at_zk],
+            dst_ref=buf_b.at[at_zk],
             send_sem=s4,
             recv_sem=r4,
-            device_id=(yy * SZ + z, xx * 2 + k),
+            device_id=over_zk(d),
             device_id_type=MESH,
         ).start()
     pltpu.make_async_copy(buf_b.at[pl.ds(0, 15)], buf_b.at[pl.ds(0, 15)], r4).wait()
-    gram_out[mine] = jnp.sum(buf_b[...], axis=0) * SCALE
+    total[...] = jnp.sum(buf_b[...], axis=0) * SCALE
 
     for d in range(1, 16):
-        zz, kk = zk_partner(d)
         pltpu.make_async_remote_copy(
-            src_ref=gram_out.at[mine],
-            dst_ref=gram_out.at[mine],
+            src_ref=total,
+            dst_ref=gram_out.at[at_xy],
             send_sem=s5,
             recv_sem=r5,
-            device_id=(y * SZ + zz, x * 2 + kk),
+            device_id=over_xy(d)[1],
             device_id_type=MESH,
         ).start()
+    own_gram = pltpu.make_async_copy(total, gram_out.at[at_xy], own_sem.at[1])
+    own_gram.start()
 
     sent = send_r.at[:, pl.ds(0, R - RL)]
     pltpu.make_async_copy(sent, sent, s1).wait()
@@ -243,6 +281,7 @@
     sent = core.at[:, :, pl.ds(0, B - BL), :]
     pltpu.make_async_copy(sent, sent, so).wait()
     own.wait()
+    own_gram.wait()
     for sem in (s3, s4, s5):
         pltpu.make_async_copy(buf_a.at[pl.ds(0, 15)], buf_a.at[pl.ds(0, 15)], sem).wait()
     got = core_out.at[pl.ds(0, R - RL)]
@@ -259,7 +298,7 @@
             jax.ShapeDtypeStruct((16, 8, 128), F32),
         ),
         in_specs=[pl.BlockSpec(memory_space=pl.ANY)] * 4,
-        out_specs=(pl.BlockSpec(memory_space=pl.ANY), pl.BlockSpec(memory_space=pltpu.VMEM)),
+        out_specs=(pl.BlockSpec(memory_space=pl.ANY), pl.BlockSpec(memory_space=pl.ANY)),
         scratch_shapes=[
             pltpu.VMEM((NY * COLS, B), F32),
             pltpu.VMEM((NZ, C), F32),
@@ -272,14 +311,16 @@
             pltpu.VMEM((16, 8, 128), F32),
             pltpu.VMEM((16, 8, 128), F32),
             pltpu.VMEM((16, 8, 128), F32),
+            pltpu.VMEM((8, 128), F32),
             pltpu.VMEM((NZ, 2 * C), BF16),
             pltpu.VMEM((2 * B, NY * COLS), BF16),
             pltpu.VMEM((2 * R * 8, S * 8), BF16),
+            pltpu.SemaphoreType.REGULAR,
             dma((3,)),
             dma((NX,)),
-            dma, dma((NX,)),
+            dma, dma((NX, RL)),
             dma, dma,
-            dma, dma, dma,
+            dma, dma, dma((2,)),
             dma, dma,
             dma, dma,
             dma, dma,

time: 56.2 us -> 50.4 us (0.90)
  Pallas kernels: 52.1 us -> 46.2 us
    pallas_call x1, Pallas kernels: 52.1 us -> 46.2 us  [body(): pl.pallas_call(kernel, out_shape=(jax.ShapeDtypeStruct((R, NX, BL, C), F3...]
where the time goes in v4:
time: 50.4 us; the launch traced here: 50.2 us
  Pallas kernels  46.2 us (92%)
  local copies, waits for them, and re-layouts  3.35 us (7%)
  between operations  0.64 us (1%)
    pallas_call x1, Pallas kernels, body(): pl.pallas_call(kernel, out_shape=(jax.ShapeDtypeStruct((R, NX, BL, C), F3...  46.2 us
    unnamed x2, local copies, waits for them, and re-layouts  3.35 us

profile of v4, /device:TPU:1, one launch (start us, length us, event | category | flops | bytes accessed | tf_op | source)
XLA Modules:
  0.0 50.2 jit_solution(4431780574735691121)
XLA Ops:
  0.6 46.2 %shard_map.59 = (f32[16,4,16,128]{3,2,1,0:T(8,128)}, f32[16,8,128]{2,1,0:T(8,128)}) custom-call(f32[32,4,32,256]{3,2,1,0:T(8,128)} %tensor.1, f32[256,128]{1,0:T(8,128)} %fy_hbm.1, f32[256,128]{1,0:T(8,128)} %fz_hbm.1, f32[16,32]{1,0:T(8,128)} %bitcast.3), custom_call_target="tpu_custom_call" | custom-call | tf_op jit(solution)/shard_map/pallas_call | solution.py:294
  46.8 1.9 %copy.8 = f32[16,4,16,128]{3,2,1,0:T(8,128)} copy(f32[16,4,16,128]{3,2,1,0:T(8,128)} %get-tuple-element.8) | data formatting | bytes 1048576
  48.7 1.5 %copy.9 = f32[128,128]{1,0:T(8,128)} copy(f32[128,128]{1,0:T(8,128)} %bitcast.2) | data formatting | bytes 131072

commit v5 on v4

--- a/solution.py
+++ b/solution.py
@@ -19,7 +19,7 @@
 BL = B // COLS
 SCALE = 1.0 / (R * B * C)
 FAR_FIRST = (4, 5, 3, 2, 6, 7, 1)
-VMEM_BYTES = 63 * 1024 * 1024
+VMEM_BYTES = 40 * 1024 * 1024
 
 
 def split(a):
@@ -289,6 +289,10 @@
     pltpu.make_async_copy(gram_out.at[pl.ds(0, 15)], gram_out.at[pl.ds(0, 15)], r5).wait()
 
 
+def in_hbm(a):
+    return pltpu.with_memory_space_constraint(a, pltpu.HBM)
+
+
 def body(tensor, factor_y, factor_z, factor_s):
     dma = pltpu.SemaphoreType.DMA
     core, gram = pl.pallas_call(
@@ -297,7 +301,7 @@
             jax.ShapeDtypeStruct((R, NX, BL, C), F32),
             jax.ShapeDtypeStruct((16, 8, 128), F32),
         ),
-        in_specs=[pl.BlockSpec(memory_space=pl.ANY)] * 4,
+        in_specs=[pl.BlockSpec(memory_space=pltpu.HBM)] * 4,
         out_specs=(pl.BlockSpec(memory_space=pl.ANY), pl.BlockSpec(memory_space=pl.ANY)),
         scratch_shapes=[
             pltpu.VMEM((NY * COLS, B), F32),
@@ -328,7 +332,7 @@
         compiler_params=pltpu.CompilerParams(
             collective_id=0, has_side_effects=True, vmem_limit_bytes=VMEM_BYTES
         ),
-    )(tensor, factor_y, factor_z, factor_s.T)
+    )(*(in_hbm(a) for a in (tensor, factor_y, factor_z, factor_s.T)))
     return core, gram.reshape(128, 128)
 
 

time: 50.4 us -> 48.2 us (0.956)
  local copies, waits for them, and re-layouts: 3.35 us -> 1.42 us
    unnamed x2, local copies, waits for them, and re-layouts: 3.35 us -> 1.42 us
where the time goes in v5:
time: 48.2 us
  Pallas kernels  46.1 us (96%)
  local copies, waits for them, and re-layouts  1.42 us (3%)
  between operations  0.64 us (1%)
    pallas_call x1, Pallas kernels, body(): pl.pallas_call(kernel, out_shape=(jax.ShapeDtypeStruct((R, NX, BL, C), F3...  46.1 us
    unnamed x2, local copies, waits for them, and re-layouts  1.42 us

profile of v5, /device:TPU:1, one launch (start us, length us, event | category | flops | bytes accessed | tf_op | source)
XLA Modules:
  0.0 48.2 jit_solution(7075011747217675508)
XLA Ops:
  0.6 46.1 %shard_map.59 = (f32[16,4,16,128]{3,2,1,0:T(8,128)S(1)}, f32[16,8,128]{2,1,0:T(8,128)S(1)}) custom-call(f32[32,4,32,256]{3,2,1,0:T(8,128)} %tensor.1, f32[256,128]{1,0:T(8,128)} %fy_hbm.1, f32[256,128]{1,0:T(8,128)} %fz_hbm.1, f32[16,32]{1,0:T(8,128)} %bitcast.3), custom_call_target="tpu_custom_call" | custom-call | tf_op jit(solution)/shard_map/pallas_call | solution.py:298
  46.7 0.8 %copy.8 = f32[16,4,16,128]{3,2,1,0:T(8,128)} copy(f32[16,4,16,128]{3,2,1,0:T(8,128)S(1)} %get-tuple-element.8) | data formatting | bytes 1048576
  47.5 0.6 %copy.9 = f32[128,128]{1,0:T(8,128)} copy(f32[128,128]{1,0:T(8,128)S(1)} %bitcast.2) | data formatting | bytes 131072

commit v6 on v5

--- a/solution.py
+++ b/solution.py
@@ -19,6 +19,8 @@
 BL = B // COLS
 SCALE = 1.0 / (R * B * C)
 FAR_FIRST = (4, 5, 3, 2, 6, 7, 1)
+XY_ORDER = (10, 6, 9, 11, 14, 2, 5, 7, 8, 13, 15, 1, 3, 4, 12)
+ZK_ORDER = (9, 8, 7, 11, 6, 10, 5, 13, 4, 12, 3, 15, 2, 14, 1)
 VMEM_BYTES = 40 * 1024 * 1024
 
 
@@ -164,6 +166,9 @@
     def block(p):
         return pl.ds(pl.multiple_of(p // RL * 8, 8), 8)
 
+    def at_row(n):
+        return pl.ds(pl.multiple_of((i * NX + n) * 8, 8), 8)
+
     for n in range(NX):
         for rank in range(RL):
             got = recv_r.at[n, rank, pl.ds(0, NY * (COLS - 1)), :]
@@ -184,7 +189,7 @@
                 def _():
                     pltpu.make_async_remote_copy(
                         src_ref=core.at[rank, n, block(p), :],
-                        dst_ref=rows.at[i * NX + n],
+                        dst_ref=rows.at[at_row(n), :],
                         send_sem=s2,
                         recv_sem=r2,
                         device_id=(p, j),
@@ -194,7 +199,7 @@
                 return 0
 
             lax.fori_loop(0, ROWS // RL, send_rows, 0)
-        rows[i * NX + n] = core[lax.rem(i, RL), n, block(i), :]
+        rows[at_row(n), :] = core[lax.rem(i, RL), n, block(i), :]
 
     for d in range(1, COLS):
         q = col_partner(d)
@@ -213,11 +218,11 @@
     )
     own.start()
 
-    got = rows.at[pl.ds(0, (ROWS - 1) * NX)]
+    got = rows.at[pl.ds(0, (ROWS - 1) * NX * 8)]
     pltpu.make_async_copy(got, got, r2).wait()
     gh, gl = [], []
     for e in range(8):
-        h, l = split(rows[:, e, :])
+        h, l = split(rows[pl.ds(e, ROWS * NX, stride=8), :])
         gh.append(h)
         gl.append(l)
     gh = jnp.concatenate(gh, axis=1)
@@ -236,7 +241,7 @@
         zz, kk = add_mod(z, d // 2, SZ), add_mod(k, d % 2, 2)
         return (y * SZ + zz, x * 2 + kk)
 
-    for d in range(1, 16):
+    for d in XY_ORDER:
         slot, device = over_xy(d)
         pltpu.make_async_remote_copy(
             src_ref=part.at[slot],
@@ -250,7 +255,7 @@
     pltpu.make_async_copy(buf_a.at[pl.ds(0, 15)], buf_a.at[pl.ds(0, 15)], r3).wait()
 
     buf_b[at_zk] = jnp.sum(buf_a[...], axis=0)
-    for d in range(1, 16):
+    for d in ZK_ORDER:
         pltpu.make_async_remote_copy(
             src_ref=buf_b.at[at_zk],
             dst_ref=buf_b.at[at_zk],
@@ -262,7 +267,7 @@
     pltpu.make_async_copy(buf_b.at[pl.ds(0, 15)], buf_b.at[pl.ds(0, 15)], r4).wait()
     total[...] = jnp.sum(buf_b[...], axis=0) * SCALE
 
-    for d in range(1, 16):
+    for d in XY_ORDER:
         pltpu.make_async_remote_copy(
             src_ref=total,
             dst_ref=gram_out.at[at_xy],
@@ -276,7 +281,7 @@
 
     sent = send_r.at[:, pl.ds(0, R - RL)]
     pltpu.make_async_copy(sent, sent, s1).wait()
-    sent = rows.at[pl.ds(0, (ROWS - 1) * NX)]
+    sent = rows.at[pl.ds(0, (ROWS - 1) * NX * 8)]
     pltpu.make_async_copy(sent, sent, s2).wait()
     sent = core.at[:, :, pl.ds(0, B - BL), :]
     pltpu.make_async_copy(sent, sent, so).wait()
@@ -311,7 +316,7 @@
             pltpu.VMEM((NX, R, NY, C), F32),
             pltpu.VMEM((NX, RL, NY * COLS, C), F32),
             pltpu.VMEM((RL, NX, B, C), F32),
-            pltpu.VMEM((ROWS * NX, 8, C), F32),
+            pltpu.VMEM((ROWS * NX * 8, C), F32),
             pltpu.VMEM((16, 8, 128), F32),
             pltpu.VMEM((16, 8, 128), F32),
             pltpu.VMEM((16, 8, 128), F32),

time: 48.2 us -> 46.2 us (0.959)
  Pallas kernels: 46.1 us -> 44.1 us
    pallas_call x1, Pallas kernels: 46.1 us -> 44.1 us  [body(): pl.pallas_call(kernel, out_shape=(jax.ShapeDtypeStruct((R, NX, BL, C), F3...]
where the time goes in v6:
time: 46.2 us
  Pallas kernels  44.1 us (95%)
  local copies, waits for them, and re-layouts  1.42 us (3%)
  between operations  0.64 us (1%)
    pallas_call x1, Pallas kernels, body(): pl.pallas_call(kernel, out_shape=(jax.ShapeDtypeStruct((R, NX, BL, C), F3...  44.1 us
    unnamed x2, local copies, waits for them, and re-layouts  1.42 us

profile of v6, /device:TPU:1, one launch (start us, length us, event | category | flops | bytes accessed | tf_op | source)
XLA Modules:
  0.0 46.2 jit_solution(9773101682730004692)
XLA Ops:
  0.6 44.1 %shard_map.59 = (f32[16,4,16,128]{3,2,1,0:T(8,128)S(1)}, f32[16,8,128]{2,1,0:T(8,128)S(1)}) custom-call(f32[32,4,32,256]{3,2,1,0:T(8,128)} %tensor.1, f32[256,128]{1,0:T(8,128)} %fy_hbm.1, f32[256,128]{1,0:T(8,128)} %fz_hbm.1, f32[16,32]{1,0:T(8,128)} %bitcast.3), custom_call_target="tpu_custom_call" | custom-call | tf_op jit(solution)/shard_map/pallas_call | solution.py:303
  44.7 0.8 %copy.8 = f32[16,4,16,128]{3,2,1,0:T(8,128)} copy(f32[16,4,16,128]{3,2,1,0:T(8,128)S(1)} %get-tuple-element.8) | data formatting | bytes 1048576
  45.5 0.6 %copy.9 = f32[128,128]{1,0:T(8,128)} copy(f32[128,128]{1,0:T(8,128)S(1)} %bitcast.2) | data formatting | bytes 131072

commit v7 on v6

--- a/solution.py
+++ b/solution.py
@@ -65,7 +65,7 @@
         pltpu.make_async_copy(a, b, f_sem.at[n])
         for n, (a, b) in enumerate(((fz_hbm, fz), (fs_hbm, fs), (fy_hbm, fy)))
     ]
-    for c in factors[:2] + loads[:1] + factors[2:] + loads[1:]:
+    for c in factors[:2] + loads + factors[2:]:
         c.start()
 
     barrier = pltpu.get_barrier_semaphore()
@@ -90,14 +90,11 @@
 
     lax.fori_loop(1, ROWS, greet_row, 0)
 
-    for c in factors:
+    for c in factors[:2]:
         c.wait()
     zh, zl = split(fz[...])
     fz_w[:, :C] = zh
     fz_w[:, C:] = zl
-    yh, yl = split(fy[...].T)
-    fy_w[:B] = yh
-    fy_w[B:] = yl
     sh, sl = split(fs[...])
     pick_r = (
         lax.broadcasted_iota(jnp.int32, (R * 8, R), 0) // 8
@@ -155,6 +152,11 @@
                     device_id_type=MESH,
                 ).start()
 
+    factors[2].wait()
+    yh, yl = split(fy[...].T)
+    fy_w[:B] = yh
+    fy_w[B:] = yl
+
     @pl.when(k == 1)
     def _():
         pl.semaphore_wait(barrier, 2 * (ROWS - 1))
@@ -292,6 +294,21 @@
     got = core_out.at[pl.ds(0, R - RL)]
     pltpu.make_async_copy(got, got, ro).wait()
     pltpu.make_async_copy(gram_out.at[pl.ds(0, 15)], gram_out.at[pl.ds(0, 15)], r5).wait()
+
+
+def place(core, gram, core_out, gram_out, sem):
+    copies = [
+        pltpu.make_async_copy(core, core_out, sem.at[0]),
+        pltpu.make_async_copy(gram, gram_out, sem.at[1]),
+    ]
+    for c in copies:
+        c.start()
+    for c in copies:
+        c.wait()
+
+
+def in_vmem(a):
+    return pltpu.with_memory_space_constraint(a, pltpu.VMEM)
 
 
 def in_hbm(a):
@@ -338,7 +355,17 @@
             collective_id=0, has_side_effects=True, vmem_limit_bytes=VMEM_BYTES
         ),
     )(*(in_hbm(a) for a in (tensor, factor_y, factor_z, factor_s.T)))
-    return core, gram.reshape(128, 128)
+    return pl.pallas_call(
+        place,
+        out_shape=(
+            jax.ShapeDtypeStruct((R, NX, BL, C), F32),
+            jax.ShapeDtypeStruct((128, 128), F32),
+        ),
+        in_specs=[pl.BlockSpec(memory_space=pltpu.VMEM)] * 2,
+        out_specs=(pl.BlockSpec(memory_space=pl.ANY), pl.BlockSpec(memory_space=pl.ANY)),
+        scratch_shapes=[dma((2,))],
+        compiler_params=pltpu.CompilerParams(vmem_limit_bytes=2 * 1024 * 1024),
+    )(core, gram.reshape(128, 128))
 
 
 def solution(mesh):

time: 46.2 us -> 45.4 us (0.983)
  local copies, waits for them, and re-layouts: 1.42 us -> 0 us
  Pallas kernels: 44.1 us -> 44.6 us
    unnamed x2 -> x0, local copies, waits for them, and re-layouts: 1.42 us -> none
    pallas_call x0 -> x1, Pallas kernels: none -> 0.82 us  [body(): pl.pallas_call(place, out_shape=(jax.ShapeDtypeStruct((R, NX, BL, C), F32...]
where the time goes in v7:
time: 45.4 us; the launch traced here: 45.3 us
  Pallas kernels  44.6 us (98%)
  between operations  0.64 us (1%)
    pallas_call x1, Pallas kernels, body(): pl.pallas_call(kernel, out_shape=(jax.ShapeDtypeStruct((R, NX, BL, C), F3...  43.8 us

profile of v7, /device:TPU:1, one launch (start us, length us, event | category | flops | bytes accessed | tf_op | source)
XLA Modules:
  0.0 45.3 jit_solution(10634807595595319349)
XLA Ops:
  0.6 43.8 %shard_map.59 = (f32[16,4,16,128]{3,2,1,0:T(8,128)S(1)}, f32[16,8,128]{2,1,0:T(8,128)S(1)}) custom-call(f32[32,4,32,256]{3,2,1,0:T(8,128)} %tensor.1, f32[256,128]{1,0:T(8,128)} %fy_hbm.1, f32[256,128]{1,0:T(8,128)} %fz_hbm.1, f32[16,32]{1,0:T(8,128)} %bitcast.3), custom_call_target="tpu_custom_call" | custom-call | tf_op jit(solution)/shard_map/pallas_call | solution.py:320
  44.5 0.8 %shard_map.60 = (f32[16,4,16,128]{3,2,1,0:T(8,128)}, f32[128,128]{1,0:T(8,128)}) custom-call(f32[16,4,16,128]{3,2,1,0:T(8,128)S(1)} %get-tuple-element.4.core, f32[128,128]{1,0:T(8,128)S(1)} %bitcast.2), custom_call_target="tpu_custom_call" | custom-call | tf_op jit(solution)/shard_map/pallas_call | solution.py:358

commit v8 on v7

--- a/solution.py
+++ b/solution.py
@@ -171,36 +171,39 @@
     def at_row(n):
         return pl.ds(pl.multiple_of((i * NX + n) * 8, 8), 8)
 
+    @pl.when(k == 0)
+    def _():
+        pl.semaphore_wait(mate_in, 1)
+
+    def finish(c, _):
+        n, rank = c // RL, lax.rem(c, RL)
+        got = recv_r.at[n, rank, pl.ds(0, NY * (COLS - 1)), :]
+        pltpu.make_async_copy(got, got, r1.at[n, rank]).wait()
+        mh, ml = split(recv_r[n, rank])
+        v = dot(fy_w[...], mh)
+        core[rank, n] = v[:B] + (v[B:] + dot(fy_w[:B], ml))
+
+        def send_rows(d, _):
+            p = lax.rem(i // RL + d, ROWS // RL) * RL + rank
+
+            @pl.when(p != i)
+            def _():
+                pltpu.make_async_remote_copy(
+                    src_ref=core.at[rank, n, block(p), :],
+                    dst_ref=rows.at[at_row(n), :],
+                    send_sem=s2,
+                    recv_sem=r2,
+                    device_id=(p, j),
+                    device_id_type=MESH,
+                ).start()
+
+            return 0
+
+        lax.fori_loop(0, ROWS // RL, send_rows, 0)
+        return 0
+
+    lax.fori_loop(0, NX * RL, finish, 0)
     for n in range(NX):
-        for rank in range(RL):
-            got = recv_r.at[n, rank, pl.ds(0, NY * (COLS - 1)), :]
-            pltpu.make_async_copy(got, got, r1.at[n, rank]).wait()
-            mh, ml = split(recv_r[n, rank])
-            v = dot(fy_w[...], mh)
-            core[rank, n] = v[:B] + (v[B:] + dot(fy_w[:B], ml))
-            if n == 0 and rank == 0:
-
-                @pl.when(k == 0)
-                def _():
-                    pl.semaphore_wait(mate_in, 1)
-
-            def send_rows(d, _, n=n, rank=rank):
-                p = lax.rem(i // RL + d, ROWS // RL) * RL + rank
-
-                @pl.when(p != i)
-                def _():
-                    pltpu.make_async_remote_copy(
-                        src_ref=core.at[rank, n, block(p), :],
-                        dst_ref=rows.at[at_row(n), :],
-                        send_sem=s2,
-                        recv_sem=r2,
-                        device_id=(p, j),
-                        device_id_type=MESH,
-                    ).start()
-
-                return 0
-
-            lax.fori_loop(0, ROWS // RL, send_rows, 0)
         rows[at_row(n), :] = core[lax.rem(i, RL), n, block(i), :]
 
     for d in range(1, COLS):

time: 45.4 us -> 45.1 us (level)
  no operation moved by 1% of the time
where the time goes in v8:
time: 45.1 us; the launch traced here: 45 us
  Pallas kernels  44.3 us (98%)
  between operations  0.64 us (1%)
    pallas_call x1, Pallas kernels, body(): pl.pallas_call(kernel, out_shape=(jax.ShapeDtypeStruct((R, NX, BL, C), F3...  43.5 us

profile of v8, /device:TPU:1, one launch (start us, length us, event | category | flops | bytes accessed | tf_op | source)
XLA Modules:
  0.0 45.0 jit_solution(3837521743535755048)
XLA Ops:
  0.6 43.5 %shard_map.59 = (f32[16,4,16,128]{3,2,1,0:T(8,128)S(1)}, f32[16,8,128]{2,1,0:T(8,128)S(1)}) custom-call(f32[32,4,32,256]{3,2,1,0:T(8,128)} %tensor.1, f32[256,128]{1,0:T(8,128)} %fy_hbm.1, f32[256,128]{1,0:T(8,128)} %fz_hbm.1, f32[16,32]{1,0:T(8,128)} %bitcast.3), custom_call_target="tpu_custom_call" | custom-call | tf_op jit(solution)/shard_map/pallas_call | solution.py:323
  44.2 0.8 %shard_map.60 = (f32[16,4,16,128]{3,2,1,0:T(8,128)}, f32[128,128]{1,0:T(8,128)}) custom-call(f32[16,4,16,128]{3,2,1,0:T(8,128)S(1)} %get-tuple-element.4.core, f32[128,128]{1,0:T(8,128)S(1)} %bitcast.2), custom_call_target="tpu_custom_call" | custom-call | tf_op jit(solution)/shard_map/pallas_call | solution.py:361

commit v9 on v8

--- a/solution.py
+++ b/solution.py
@@ -39,7 +39,7 @@
 
 
 def add_mod(a, d, n):
-    return lax.rem(a + d, n)
+    return jnp.where(a + d < n, a + d, a + d - n)
 
 
 def kernel(
@@ -113,8 +113,8 @@
         fs_w[at : at + R * 8] = jnp.where(same, wide, 0.0).astype(BF16)
 
     mine_y = pl.ds(pl.multiple_of(j * NY, NY), NY)
-    for n in range(NX):
-        loads[n].wait()
+    def contract(n):
+        pltpu.make_async_copy(tensor.at[:, n], tbuf.at[n], t_sem.at[n]).wait()
         for h in range(2):
             t = tbuf[n, :, 16 * h : 16 * h + 16, :].reshape(S * 16, NZ)
             th, tl = split(t)
@@ -129,17 +129,8 @@
                 send_r[n, :, 16 * h + 8 * g : 16 * h + 8 * g + 8, :] = v[
                     :, g * C : (g + 1) * C
                 ].reshape(R, 8, C)
-        if n == 0:
-
-            @pl.when(k == 0)
-            def _():
-                pl.semaphore_wait(barrier, COLS - 1)
-                pl.semaphore_signal(mate_in, inc=1, device_id=(i, j + 1), device_id_type=MESH)
-
-            @pl.when(k == 1)
-            def _():
-                pl.semaphore_wait(mate_in, 1)
-
+
+    def send_ranks(n):
         for rank in range(RL):
             for d in FAR_FIRST:
                 q = col_partner(d)
@@ -152,6 +143,26 @@
                     device_id_type=MESH,
                 ).start()
 
+    contract(0)
+
+    @pl.when(k == 0)
+    def _():
+        pl.semaphore_wait(barrier, COLS - 1)
+        pl.semaphore_signal(mate_in, inc=1, device_id=(i, j + 1), device_id_type=MESH)
+
+    @pl.when(k == 1)
+    def _():
+        pl.semaphore_wait(mate_in, 1)
+
+    send_ranks(0)
+
+    def rest(n, _):
+        contract(n)
+        send_ranks(n)
+        return 0
+
+    lax.fori_loop(1, NX, rest, 0)
+
     factors[2].wait()
     yh, yl = split(fy[...].T)
     fy_w[:B] = yh
@@ -184,12 +195,13 @@
         core[rank, n] = v[:B] + (v[B:] + dot(fy_w[:B], ml))
 
         def send_rows(d, _):
-            p = lax.rem(i // RL + d, ROWS // RL) * RL + rank
+            slot = add_mod(i // RL, d, ROWS // RL)
+            p = slot * RL + rank
 
             @pl.when(p != i)
             def _():
                 pltpu.make_async_remote_copy(
-                    src_ref=core.at[rank, n, block(p), :],
+                    src_ref=core.at[rank, n, pl.ds(pl.multiple_of(slot * 8, 8), 8), :],
                     dst_ref=rows.at[at_row(n), :],
                     send_sem=s2,
                     recv_sem=r2,

time: 45.1 us -> 45 us (level)
  no operation moved by 1% of the time
where the time goes in v9:
time: 45 us; the launch traced here: 44.9 us
  Pallas kernels  44.3 us (98%)
  between operations  0.64 us (1%)
    pallas_call x1, Pallas kernels, body(): pl.pallas_call(kernel, out_shape=(jax.ShapeDtypeStruct((R, NX, BL, C), F3...  43.5 us

profile of v9, /device:TPU:1, one launch (start us, length us, event | category | flops | bytes accessed | tf_op | source)
XLA Modules:
  0.0 44.9 jit_solution(15656295777639567385)
XLA Ops:
  0.6 43.5 %shard_map.59 = (f32[16,4,16,128]{3,2,1,0:T(8,128)S(1)}, f32[16,8,128]{2,1,0:T(8,128)S(1)}) custom-call(f32[32,4,32,256]{3,2,1,0:T(8,128)} %tensor.1, f32[256,128]{1,0:T(8,128)} %fy_hbm.1, f32[256,128]{1,0:T(8,128)} %fz_hbm.1, f32[16,32]{1,0:T(8,128)} %bitcast.3), custom_call_target="tpu_custom_call" | custom-call | tf_op jit(solution)/shard_map/pallas_call | solution.py:335
  44.1 0.8 %shard_map.60 = (f32[16,4,16,128]{3,2,1,0:T(8,128)}, f32[128,128]{1,0:T(8,128)}) custom-call(f32[16,4,16,128]{3,2,1,0:T(8,128)S(1)} %get-tuple-element.4.core, f32[128,128]{1,0:T(8,128)S(1)} %bitcast.2), custom_call_target="tpu_custom_call" | custom-call | tf_op jit(solution)/shard_map/pallas_call | solution.py:373

commit v10 on v9

--- a/solution.py
+++ b/solution.py
@@ -182,10 +182,6 @@
     def at_row(n):
         return pl.ds(pl.multiple_of((i * NX + n) * 8, 8), 8)
 
-    @pl.when(k == 0)
-    def _():
-        pl.semaphore_wait(mate_in, 1)
-
     def finish(c, _):
         n, rank = c // RL, lax.rem(c, RL)
         got = recv_r.at[n, rank, pl.ds(0, NY * (COLS - 1)), :]
@@ -193,6 +189,10 @@
         mh, ml = split(recv_r[n, rank])
         v = dot(fy_w[...], mh)
         core[rank, n] = v[:B] + (v[B:] + dot(fy_w[:B], ml))
+
+        @pl.when((k == 0) & (c == 0))
+        def _():
+            pl.semaphore_wait(mate_in, 1)
 
         def send_rows(d, _):
             slot = add_mod(i // RL, d, ROWS // RL)

time: 45 us -> 45 us (level)
  no operation moved by 1% of the time
where the time goes in v10:
time: 45 us
  Pallas kernels  44.3 us (98%)
  between operations  0.64 us (1%)
    pallas_call x1, Pallas kernels, body(): pl.pallas_call(kernel, out_shape=(jax.ShapeDtypeStruct((R, NX, BL, C), F3...  43.5 us

profile of v10, /device:TPU:1, one launch (start us, length us, event | category | flops | bytes accessed | tf_op | source)
XLA Modules:
  0.0 45.0 jit_solution(228750770157630559)
XLA Ops:
  0.6 43.5 %shard_map.59 = (f32[16,4,16,128]{3,2,1,0:T(8,128)S(1)}, f32[16,8,128]{2,1,0:T(8,128)S(1)}) custom-call(f32[32,4,32,256]{3,2,1,0:T(8,128)} %tensor.1, f32[256,128]{1,0:T(8,128)} %fy_hbm.1, f32[256,128]{1,0:T(8,128)} %fz_hbm.1, f32[16,32]{1,0:T(8,128)} %bitcast.3), custom_call_target="tpu_custom_call" | custom-call | tf_op jit(solution)/shard_map/pallas_call | solution.py:335
  44.1 0.8 %shard_map.60 = (f32[16,4,16,128]{3,2,1,0:T(8,128)}, f32[128,128]{1,0:T(8,128)}) custom-call(f32[16,4,16,128]{3,2,1,0:T(8,128)S(1)} %get-tuple-element.4.core, f32[128,128]{1,0:T(8,128)S(1)} %bitcast.2), custom_call_target="tpu_custom_call" | custom-call | tf_op jit(solution)/shard_map/pallas_call | solution.py:373
